TPU v7x, 256 devices: a whole 4x4x8 slice. The times are simulated.
256 devices in a mesh: store: 16 (over z, core), cand: 16 (over x, y).
Axes of the slice: x: 4, y: 4, z: 8, core: 2. Of those that a mesh axis runs over, the one named last changes fastest.
Arguments:
- kv_cache: bfloat16 [256, 2, 1024, 2048], P('store', None, 'cand'), may hold values from -6 to 6
- requests: int32 [256], P('store'), may hold values from 0 to 15, as said below
- lengths: int32 [256], P('store'), may hold values from 128 to 1024, as said below
- cand_feats: bfloat16 [256, 384, 1024], P('store', 'cand'), may hold values from -6 to 6
- w_in: bfloat16 [2, 1024, 4096], P(None, None, 'cand'), may hold values from -0.1875 to 0.1875
- w_out: bfloat16 [2, 1024, 1024], P(None, None, 'cand'), may hold values from -0.1875 to 0.1875
Outputs:
- ranked: bfloat16 [256, 384, 1024], P('store', 'cand')
Inputs may be any that keep to these rules, and one draw needn't show every extreme that they name: `requests`: among the 16 users of one store index, every scorer index appears exactly 1 times. `lengths`: multiples of 128; some slot has 1024.
All inputs are finite; a program needn't handle non-finite values.
Results may differ from a plain program's by a relative error of at most 0.011.
Values may be sent and summed in bfloat16 or wider, within the bound.
A program may use at most 128 MiB of HBM per device.

v0:
```python
import jax
import jax.numpy as jnp
from jax import lax
from jax.sharding import PartitionSpec as P

HEADS = 8


def layer_norm(values):
    mean = jnp.mean(values, axis=-1, keepdims=True)
    centred = values - mean
    spread = jnp.mean(centred * centred, axis=-1, keepdims=True)
    return centred * lax.rsqrt(spread + 1e-06)


def attend(mixed, cache, live_len, group, cands, width):
    heads = HEADS
    head = width // heads
    scale = head ** (-0.5)
    history = cache.shape[1]
    gate = mixed[:, :width]
    value = mixed[:, width : 2 * width].astype(jnp.bfloat16).reshape(group, cands, heads, head)
    query = mixed[:, 2 * width : 3 * width].astype(jnp.bfloat16).reshape(group, cands, heads, head)
    own_key = mixed[:, 3 * width :].astype(jnp.bfloat16).reshape(group, cands, heads, head)
    past_key = cache[:, :, :width].reshape(group, history, heads, head)
    past_value = cache[:, :, width:].reshape(group, history, heads, head)
    scores = (
        jnp.einsum("gchd,gjhd->ghcj", query, past_key, preferred_element_type=jnp.float32) * scale
    )
    live = (jnp.arange(history, dtype=jnp.int32)[None, :] < live_len[:, None]).astype(jnp.float32)
    weights = (jax.nn.silu(scores) * live[:, None, None, :]).astype(jnp.bfloat16)
    attended = jnp.einsum(
        "ghcj,gjhd->gchd", weights, past_value, preferred_element_type=jnp.float32
    )
    own = jax.nn.silu(
        jnp.einsum("gchd,gchd->gch", query, own_key, preferred_element_type=jnp.float32) * scale
    )
    attended = attended + own[..., None] * value.astype(jnp.float32)
    attended = attended.reshape(group * cands, width)
    return (layer_norm(attended) * gate).astype(jnp.bfloat16)


def shards(kv_cache, requests, lengths, cand_feats, w_in, w_out):
    n_store = lax.axis_size("store")
    n_cand = lax.axis_size("cand")
    owned = requests.shape[0]
    per_pair = owned // n_store
    group = owned // n_cand
    local = jnp.arange(owned, dtype=jnp.int32)
    same = (requests[:, None] == requests[None, :]) & (local[None, :] < local[:, None])
    rank = jnp.sum(same.astype(jnp.int32), axis=1)
    target = requests * per_pair + rank
    order = jnp.sum(jnp.where(target[:, None] == local[None, :], local[:, None], 0), axis=0)
    outgoing = jnp.take(kv_cache, order, axis=0)
    histories = lax.all_to_all(
        lax.all_to_all(outgoing, "store", split_axis=0, concat_axis=0, tiled=True),
        "cand",
        split_axis=0,
        concat_axis=2,
        tiled=True,
    )
    start = lax.axis_index("cand") * group
    live_len = lax.dynamic_slice_in_dim(lengths, start, group)
    rows = lax.all_to_all(cand_feats, "cand", split_axis=0, concat_axis=1, tiled=True)
    cands = rows.shape[1]
    width = rows.shape[2]
    state = rows.reshape(group * cands, width).astype(jnp.float32)
    for layer in range(w_in.shape[0]):
        cache = histories[:, layer]
        normed = layer_norm(state).astype(jnp.bfloat16)
        mixed = jax.nn.silu(
            jnp.dot(
                normed,
                lax.all_gather(w_in[layer], "cand", axis=1, tiled=True),
                preferred_element_type=jnp.float32,
            )
        )
        gated = attend(mixed, cache, live_len, group, cands, width)
        update = jnp.dot(
            gated,
            lax.all_gather(w_out[layer], "cand", axis=1, tiled=True),
            preferred_element_type=jnp.float32,
        )
        state = state + update
    result = state.reshape(group, cands, width).astype(jnp.bfloat16)
    return lax.all_to_all(result, "cand", split_axis=1, concat_axis=0, tiled=True)


def solution(mesh):
    return jax.shard_map(
        shards,
        mesh=mesh,
        in_specs=(
            P("store", None, "cand", None),
            P("store"),
            P("store"),
            P("store", "cand", None),
            P(None, None, "cand"),
            P(None, None, "cand"),
        ),
        out_specs=P("store", "cand", None),
        check_vma=False,
    )
```

profile of v0, /device:TPU:32, one launch (start us, length us, event | category | flops | bytes accessed | tf_op | source)
XLA Modules:
  0.0 500.7 jit_solution(15039722262324925976)
XLA Ops:
  8.8 7.0 %all-to-all-start = ((bf16[16,24,1024]{2,1,0:T(8,128)(2,1)}), bf16[16,24,1024]{2,1,0:T(8,128)(2,1)S(1)}, u32[]{:S(2)}, u32[]{:S(2)}) async-start(bf16[16,24,1024]{2,1,0:T(8,128)(2,1)} %param.9), calls=%async_computation | async-start | bytes 1572864 | tf_op jit(solution)/shard_map/all_to_all | solution.py:64
  16.2 8.2 %gather_fusion = bf16[16,2,64,2048]{3,2,1,0:T(8,128)(2,1)} fusion(bf16[16,2,64,2048]{3,2,1,0:T(8,128)(2,1)} %param.6, s32[1024]{0:T(1024)S(1)} %pad_clamp_fusion), kind=kCustom, calls=%fused_computation | custom fusion | bytes 16777280 | tf_op jit(solution)/shard_map/jit(_take)/gather | solution.py:54
  24.4 7.8 %broadcast_select_fusion = bf16[16,2,64,2048]{3,2,1,0:T(8,128)(2,1)} fusion(bf16[16,2,64,2048]{3,2,1,0:T(8,128)(2,1)} %gather_fusion, pred[16]{0:T(512)(128)(4,1)S(1)} %compare_and_fusion), kind=kLoop, calls=%fused_computation.7 | loop fusion | flops 4194304 | bytes 16777232 | tf_op jit(solution)/shard_map/jit(_take)/select_n | solution.py:54
  32.2 8.6 %all-to-all-start.1 = ((bf16[16,2,64,2048]{3,2,1,0:T(8,128)(2,1)}), bf16[16,2,64,2048]{3,2,1,0:T(8,128)(2,1)}, u32[]{:S(2)}, u32[]{:S(2)}) async-start(bf16[16,2,64,2048]{3,2,1,0:T(8,128)(2,1)} %broadcast_select_fusion), calls=%async_computation.1 | async-start | bytes 16777216 | tf_op jit(solution)/shard_map/all_to_all | solution.py:56
  42.3 180.9 %all-to-all-done.1 = bf16[16,2,64,2048]{3,2,1,0:T(8,128)(2,1)} async-done(((bf16[16,2,64,2048]{3,2,1,0:T(8,128)(2,1)}), bf16[16,2,64,2048]{3,2,1,0:T(8,128)(2,1)}, u32[]{:S(2)}, u32[]{:S(2)}) %all-to-all-start.1) | async-done | bytes 8388640 | tf_op jit(solution)/shard_map/all_to_all | solution.py:56
  223.2 7.2 %all-to-all-start.2 = ((bf16[16,2,64,2048]{3,2,1,0:T(8,128)(2,1)}), bf16[16,2,64,2048]{3,2,1,0:T(8,128)(2,1)}, u32[]{:S(2)}, u32[]{:S(2)}) async-start(bf16[16,2,64,2048]{3,2,1,0:T(8,128)(2,1)} %all-to-all-done.1), calls=%async_computation.2 | async-start | bytes 16777216 | tf_op jit(solution)/shard_map/all_to_all | solution.py:55
  233.3 8.9 %fusion.60 = (bf16[384,4096]{1,0:T(8,128)(2,1)S(1)}, f32[384,4096]{1,0:T(8,128)}) fusion(bf16[384,1024]{1,0:T(8,128)(2,1)S(1)} %fusion.25, bf16[1,1024,4096]{2,1,0:T(8,128)(2,1)} %all-gather.9.cloned.1.call-done), kind=kOutput, calls=%fused_computation.92 | convolution fusion | flops 3229089792 | bytes 18612224 | tf_op jit(solution)/shard_map/dot_general | solution.py:72
  246.2 122.8 %all-to-all-done.2 = bf16[16,2,64,2048]{3,2,1,0:T(8,128)(2,1)} async-done(((bf16[16,2,64,2048]{3,2,1,0:T(8,128)(2,1)}), bf16[16,2,64,2048]{3,2,1,0:T(8,128)(2,1)}, u32[]{:S(2)}, u32[]{:S(2)}) %all-to-all-start.2) | async-done | bytes 8388640 | tf_op jit(solution)/shard_map/all_to_all | solution.py:55
  369.0 8.3 %copy.66 = bf16[1,2,16,64,2048]{4,3,2,1,0:T(8,128)(2,1)} copy(bf16[1,2,16,64,2048]{4,3,1,2,0:T(8,128)(2,1)} %bitcast.4) | data formatting | bytes 16777216 | tf_op jit(solution)/shard_map/all_to_all | solution.py:55
  377.3 4.0 slice_bitcast_fusion
  381.3 2.9 fusion.56
  384.2 3.9 copy.67
  388.2 3.0 copy.68
  391.2 9.2 %fusion.61 = (f32[384]{0:T(512)S(1)}, f32[1,384,8,128]{1,3,2,0:T(8,128)S(1)}) fusion(f32[1,384,8,128]{1,3,2,0:T(8,128)} %bitcast.117, f32[384,8]{0,1:T(8,128)S(1)} %divide_multiply_fusion.3, bf16[1024,8,128]{0,2,1:T(8,128)(2,1)} %bitcast.115, f32[1024]{0:T(1024)S(1)} %fusion.50, bf16[1024,8,128]{0,2,1:T(8,128)(2,1)} %bitcast.116, ...), kind=kOutput, calls=%fused_computation.93 | convolution fusion | flops 1633812096 | bytes 8144384 | tf_op jit(solution)/shard_map/ghcj,gjhd->gchd/dot_general | solution.py:32
  402.4 3.7 fusion.64
  406.4 9.2 %fusion.65 = (bf16[384,4096]{1,0:T(8,128)(2,1)S(1)}, f32[384,4096]{1,0:T(8,128)}) fusion(bf16[1,1024,4096]{2,1,0:T(8,128)(2,1)} %all-gather.13.cloned.1.call-done, f32[384,1024]{1,0:T(8,128)S(1)} %get-tuple-element.28, f32[384]{0:T(512)S(1)} %add_rsqrt_fusion.2, f32[384]{0:T(512)S(1)} %broadcast_multiply_fusion.2), kind=kOutput, calls=%fused_computation.95 | convolution fusion | flops 3230269440 | bytes 19401728 | tf_op jit(solution)/shard_map/dot_general | solution.py:72
  418.3 3.1 copy.96
  421.3 4.0 copy.73
  425.3 4.1 copy.74
  429.4 10.2 %fusion.66 = (f32[384]{0:T(512)S(1)}, f32[1,384,8,128]{1,3,2,0:T(8,128)}) fusion(f32[1,384,8,128]{1,3,2,0:T(8,128)} %bitcast.118, f32[384,8]{0,1:T(8,128)S(1)} %divide_multiply_fusion.2, bf16[1024,8,128]{0,2,1:T(8,128)(2,1)} %bitcast.113, f32[1024]{0:T(1024)S(1)} %fusion.50, bf16[1024,8,128]{0,2,1:T(8,128)(2,1)} %bitcast.114, ...), kind=kOutput, calls=%fused_computation.96 | convolution fusion | flops 1633812096 | bytes 8144384 | tf_op jit(solution)/shard_map/ghcj,gjhd->gchd/dot_general | solution.py:32
  439.6 3.0 copy.97
  444.3 3.6 fusion.30
  449.6 5.4 %reduce.16 = bf16[384,1024]{1,0:T(8,128)(2,1)S(1)} reduce(bf16[384,1,1024]{2,1,0:T(2,128)(2,1)S(1)} %bitcast.107, bf16[]{:T(256)} %broadcast.226), dimensions={1}, to_apply=%bitcast.103.reduce_sub_computation | reduce | bytes 1572866
  455.6 36.4 %all_to_all.44 = bf16[16,2,12288]{2,1,0:T(2,128)(2,1)S(1)} all-to-all(bf16[16,2,12288]{2,1,0:T(2,128)(2,1)S(1)} %reshape.304), channel_id=1, replica_groups=mesh['store'=16,'cand'=16] {'cand'}, dimensions={0} | all-to-all | bytes 1572864 | tf_op jit(solution)/shard_map/all_to_all | solution.py:86
  (64 shorter events, 21.5 us)
Async XLA Ops:
  6.5 9.3 %copy-start.1 = (s32[16]{0:T(128)S(1)}, s32[16]{0:T(128)}, u32[]{:S(2)}) copy-start(s32[16]{0:T(128)} %param.7) | copy-start | bytes 196
  6.5 226.8 %all-gather.9.cloned.1.call-start = ((), (), s32[]{:S(2)}) async-start(), calls=%async_computation.4 | async-start | bytes 8912896 | tf_op jit(solution)/shard_map/all_gather | solution.py:74
  8.8 23.4 %all-to-all-start = ((bf16[16,24,1024]{2,1,0:T(8,128)(2,1)}), bf16[16,24,1024]{2,1,0:T(8,128)(2,1)S(1)}, u32[]{:S(2)}, u32[]{:S(2)}) async-start(bf16[16,24,1024]{2,1,0:T(8,128)(2,1)} %param.9), calls=%async_computation | async-start | bytes 1572864 | tf_op jit(solution)/shard_map/all_to_all | solution.py:64
  32.2 8.6 %copy-start = (bf16[2,1024,64]{1,2,0:T(8,128)(2,1)S(1)}, bf16[2,1024,64]{1,2,0:T(8,128)(2,1)}, u32[]{:S(2)}) copy-start(bf16[2,1024,64]{1,2,0:T(8,128)(2,1)} %param.11) | copy-start | bytes 786436
  32.2 191.0 %all-to-all-start.1 = ((bf16[16,2,64,2048]{3,2,1,0:T(8,128)(2,1)}), bf16[16,2,64,2048]{3,2,1,0:T(8,128)(2,1)}, u32[]{:S(2)}, u32[]{:S(2)}) async-start(bf16[16,2,64,2048]{3,2,1,0:T(8,128)(2,1)} %broadcast_select_fusion), calls=%async_computation.1 | async-start | bytes 16777216 | tf_op jit(solution)/shard_map/all_to_all | solution.py:56
  40.8 361.6 %all-gather.11.cloned.1.call-start = ((), (), s32[]{:S(2)}) async-start(), calls=%async_computation.5 | async-start | bytes 2228224 | tf_op jit(solution)/shard_map/all_gather | solution.py:81
  41.6 364.8 %all-gather.13.cloned.1.call-start = ((), (), s32[]{:S(2)}) async-start(), calls=%async_computation.6 | async-start | bytes 8912896 | tf_op jit(solution)/shard_map/all_gather | solution.py:74
  42.3 188.7 %copy-start.2 = (s32[16]{0:T(128)S(1)}, s32[16]{0:T(128)}, u32[]{:S(2)}) copy-start(s32[16]{0:T(128)} %param.8) | copy-start | bytes 196
  223.2 145.8 %all-to-all-start.2 = ((bf16[16,2,64,2048]{3,2,1,0:T(8,128)(2,1)}), bf16[16,2,64,2048]{3,2,1,0:T(8,128)(2,1)}, u32[]{:S(2)}, u32[]{:S(2)}) async-start(bf16[16,2,64,2048]{3,2,1,0:T(8,128)(2,1)} %all-to-all-done.1), calls=%async_computation.2 | async-start | bytes 16777216 | tf_op jit(solution)/shard_map/all_to_all | solution.py:55
  230.4 213.9 %all-gather.15.cloned.1.call-start = ((), (), s32[]{:S(2)}) async-start(), calls=%async_computation.7 | async-start | bytes 2228224 | tf_op jit(solution)/shard_map/all_gather | solution.py:81
Sparse Core Ops, SparseCore 0:
  9.8 86.5 all-gather.8
  98.7 49.3 all-gather.10
  150.6 82.7 all-gather.12
  235.7 142.9 all-gather.14
where the time goes:
time: 509 us; the launch traced here: 501 us
  waiting for transfers between devices  305 us (60%)
  local copies, waits for them, and re-layouts  56.6 us (11%)
  matrix products  44.8 us (9%)
  blocking collectives  36.4 us (7%)
  starting transfers between devices  23 us (5%)
  other arithmetic  21.2 us (4%)
  between operations  13.6 us (3%)
    all_to_all x1, waiting for transfers between devices, shards(): lax.all_to_all(outgoing, 'store', split_axis=0, concat_axis=0, tiled=True)  181 us
    all_to_all x1, waiting for transfers between devices, shards(): lax.all_to_all(lax.all_to_all(outgoing, 'store', split_axis=0, concat_axi...  123 us
    all_to_all x1, blocking collectives, shards(): lax.all_to_all(result, 'cand', split_axis=1, concat_axis=0, tiled=True)  36.4 us
    dot_general x2, matrix products, attend(): jnp.einsum('ghcj,gjhd->gchd', weights, past_value, preferred_element_type...  19.4 us
    dot_general x2, matrix products, shards(): jnp.dot(normed, lax.all_gather(w_in[layer], 'cand', axis=1, tiled=True),...  18.2 us
  transfers between devices with their start and end apart: 7, of which 2 were waited for; matrix products, arithmetic and copies ran while one was open for 21% of the time, Pallas kernels for 0%

commit v1 on v0

v1 whole, which is shorter than its diff:
```python
import functools

import jax
import jax.numpy as jnp
from jax import lax
from jax.experimental import pallas as pl
from jax.experimental.pallas import tpu as pltpu
from jax.sharding import PartitionSpec as P

MESH = pl.DeviceIdType.MESH
HEADS = 8
HEAD = 128
SIDE = 4
DEPTH = 8
CORES = 2
F32 = jnp.float32
BF16 = jnp.bfloat16

PLANE = (
    ((1, 0), (3, 0), (0, 1), (0, 3))
    + ((1, 1), (3, 3), (1, 3), (3, 1))
    + ((2, 2), (2, 0), (0, 2))
    + ((2, 1), (2, 3), (1, 2), (3, 2))
)
COLUMN = tuple((dz, dk) for dz in (4, 3, 5, 2, 6, 1, 7) for dk in (0, 1)) + ((0, 1),)


def layer_norm(values):
    mean = jnp.mean(values, axis=-1, keepdims=True)
    centred = values - mean
    spread = jnp.mean(centred * centred, axis=-1, keepdims=True)
    return centred * lax.rsqrt(spread + 1e-06)


def silu_of_double(half):
    return half + half * jnp.tanh(half)


def fold(rows):
    half = rows.shape[1] // 2
    return jnp.concatenate([rows[:, :half], rows[:, half:]], axis=0)


def unfold(piece):
    half = piece.shape[0] // 2
    return jnp.concatenate([piece[:half], piece[half:]], axis=1)


def arrived(region, sem):
    pltpu.make_async_copy(region, region, sem).wait()


def kernel(
    requests,
    lengths,
    kv_hbm,
    feats,
    win_hbm,
    wout_hbm,
    out,
    win,
    wout,
    kv,
    state,
    normed,
    gate,
    mixed,
    attended,
    len_out,
    len_in,
    feat_out,
    feat_in,
    feat_mid,
    feat_here,
    rank_out,
    rank_mid,
    rank_send,
    rank_in,
    inverse,
    send,
    recv,
    z_send,
    z_recv,
    twin_send,
    twin_recv,
):
    me_s = lax.axis_index("store")
    me_c = lax.axis_index("cand")
    z, core = me_s // CORES, lax.rem(me_s, CORES)
    x, y = me_c // SIDE, lax.rem(me_c, SIDE)
    layers, history, _ = kv.shape
    cands, width = state.shape
    users = kv_hbm.shape[0]
    part = cands // users
    rows = history // users
    wide = win.shape[3]
    narrow = wout_hbm.shape[1]

    plane = [
        lax.rem(x + dx, SIDE) * SIDE + lax.rem(y + dy, SIDE) for dx, dy in PLANE
    ]
    column = [
        lax.rem(z + dz, DEPTH) * CORES + lax.rem(core + dk, CORES) for dz, dk in COLUMN
    ]
    barrier = pltpu.get_barrier_semaphore()
    for c in plane:
        pl.semaphore_signal(barrier, inc=1, device_id=(me_s, c), device_id_type=MESH)
    for s in column:
        pl.semaphore_signal(barrier, inc=1, device_id=(s, me_c), device_id_type=MESH)
    for o in range(users):
        len_out[o] = jnp.full((8, 128), lengths[o], jnp.int32)
    for m in range(users // 2):
        both = feats[2 * part * m : 2 * part * (m + 1), :].astype(F32)
        for i in range(2):
            feat_out[2 * m + i] = fold(both[part * i : part * (i + 1)]).astype(BF16)
    pl.semaphore_wait(barrier, len(plane) + len(column))

    def post(src, dst, device, send_sem, recv_sem):
        pltpu.make_async_remote_copy(
            src, dst, send_sem, recv_sem, device_id=device, device_id_type=MESH
        ).start()

    def here(src, dst, sem):
        pltpu.make_async_copy(src, dst, sem).start()

    FEAT_Z, LEN_Z, FEAT_P, RANK_P, RANK_Z, IN0, WO, IN1, KV0, KV1 = range(10)

    depth = width // SIDE // CORES
    quarter = lax.rem(z, SIDE)

    def span(q, k):
        return pl.ds(pl.multiple_of((q * CORES + k) * depth, depth), depth)

    mine = span(quarter, core)
    cols_here = pl.ds(pl.multiple_of(me_c * narrow, narrow), narrow)
    rows_here = pl.ds(pl.multiple_of(me_c * rows, rows), rows)

    for s in column:
        post(feat_out.at[s], feat_in.at[me_s], (s, me_c), send.at[FEAT_Z], recv.at[FEAT_Z])
    here(feat_out.at[me_s], feat_in.at[me_s], recv.at[FEAT_Z])
    for s in column:
        post(len_out.at[s], len_in.at[me_s], (s, me_c), send.at[LEN_Z], recv.at[LEN_Z])
    here(len_out.at[me_s], len_in.at[me_s], recv.at[LEN_Z])

    def spread_in(layer, number):
        src, dst = win_hbm.at[layer, mine], win.at[layer, me_c, mine]
        for c in plane:
            post(src, dst, (me_s, c), send.at[number], recv.at[number])
        here(src, dst, recv.at[number])

    def spread_out():
        src, dst = wout_hbm.at[:, :, mine], wout.at[:, cols_here, mine]
        for c in plane:
            post(src, dst, (me_s, c), send.at[WO], recv.at[WO])
        here(src, dst, recv.at[WO])

    def histories(layer, number):
        dst = kv.at[layer, rows_here]
        for c in plane:
            post(kv_hbm.at[c, layer], dst, (me_s, c), send.at[number], recv.at[number])
        here(kv_hbm.at[me_c, layer], dst, recv.at[number])

    spread_in(0, IN0)
    spread_out()
    spread_in(1, IN1)
    histories(0, KV0)

    arrived(feat_in, recv.at[FEAT_Z])
    for k in range(users):
        feat_mid[k] = feat_in[requests[k]]
    for c in plane:
        post(feat_mid.at[c], feat_here.at[me_c], (me_s, c), send.at[FEAT_P], recv.at[FEAT_P])
    here(feat_mid.at[me_c], feat_here.at[me_c], recv.at[FEAT_P])

    half = users // 2
    up1, down1 = lax.rem(z + 1, DEPTH), lax.rem(z + DEPTH - 1, DEPTH)
    up2, down2 = lax.rem(z + 2, DEPTH), lax.rem(z + DEPTH - 2, DEPTH)

    def in_block(layer, q, k, part_of):
        if part_of is None:
            return win.at[layer, :, span(q, k)]
        return win.at[layer, pl.ds(part_of * half, half), span(q, k)]

    def out_block(_, q, k, part_of):
        if part_of is None:
            return wout.at[:, :, span(q, k)]
        return wout.at[:, pl.ds(part_of * (width // 2), width // 2), span(q, k)]

    def along_z(block, layer, group):
        for i, (to, part_of) in enumerate(
            ((up1, None), (down1, None), (up2, 0), (down2, 1))
        ):
            ref = block(layer, quarter, core, part_of)
            post(ref, ref, (to * CORES + core, me_c), z_send.at[group, i], z_recv.at[group, i])
        to_twin(block(layer, quarter, core, None), group, 0)

    def to_twin(ref, group, i):
        post(ref, ref, (z * CORES + 1 - core, me_c), twin_send.at[group, i], twin_recv.at[group, i])

    def z_blocks(block, layer):
        return [
            block(layer, lax.rem(quarter + step, SIDE), core, part_of)
            for step, part_of in ((3, None), (1, None), (2, 0), (2, 1))
        ]

    def pass_on(block, layer, group):
        for i, ref in enumerate(z_blocks(block, layer)):
            arrived(ref, z_recv.at[group, i])
            to_twin(ref, group, i + 1)

    def from_twin(block, layer, group):
        other = 1 - core
        refs = [block(layer, quarter, other, None)] + [
            block(layer, lax.rem(quarter + step, SIDE), other, part_of)
            for step, part_of in ((3, None), (1, None), (2, 0), (2, 1))
        ]
        for i, ref in enumerate(refs):
            arrived(ref, twin_recv.at[group, i])

    def sent(block, layer, group):
        for i, part_of in enumerate((None, None, 0, 1)):
            arrived(block(layer, quarter, core, part_of), z_send.at[group, i])
        for i, part_of in enumerate((None, None, None, 0, 1)):
            arrived(block(layer, quarter, core, part_of), twin_send.at[group, i])

    arrived(win.at[0, :, mine], recv.at[IN0])
    along_z(in_block, 0, 0)
    arrived(wout.at[:, :, mine], recv.at[WO])
    along_z(out_block, 0, 1)

    for s in range(users):
        at = 0
        for k in range(users):
            at = jnp.where(requests[k] == s, k, at)
        inverse[s] = at

    arrived(feat_here, recv.at[FEAT_P])
    histories(1, KV1)
    for j in range(users):
        state[part * j : part * (j + 1), :] = unfold(feat_here[j].astype(F32))

    block_rows = 32

    def norm_state():
        def step(i, _):
            at = pl.ds(pl.multiple_of(i * block_rows, block_rows), block_rows)
            normed[at, :] = layer_norm(state[at, :]).astype(BF16)
            return 0

        lax.fori_loop(0, cands // block_rows, step, 0)

    def project(layer):
        blocks = width // wide

        def gates(j, _):
            acc = jnp.dot(normed[...], win[layer, j], preferred_element_type=F32)
            at = pl.ds(pl.multiple_of(j * wide, wide), wide)
            gate[:, at] = silu_of_double(0.5 * acc)
            return 0

        lax.fori_loop(0, blocks, gates, 0)

        def others(j, _):
            acc = jnp.dot(normed[...], win[layer, j + blocks], preferred_element_type=F32)
            mixed[j] = silu_of_double(0.5 * acc).astype(BF16)
            return 0

        lax.fori_loop(0, 3 * blocks, others, 0)

    scale = HEAD ** (-0.5)
    pairs = width // wide
    tall = 128

    def attend(layer, live):
        def pair(p, _):
            for i in range(wide // HEAD):
                lanes = slice(i * HEAD, (i + 1) * HEAD)
                at = pl.ds(pl.multiple_of(p * wide + i * HEAD, HEAD), HEAD)
                at_value = pl.ds(pl.multiple_of(width + p * wide + i * HEAD, HEAD), HEAD)
                past_key = kv[layer, :, at]
                past_value = kv[layer, :, at_value]
                for t in range(cands // tall):
                    these = slice(t * tall, (t + 1) * tall)
                    value = mixed[p, these, lanes]
                    query = mixed[p + pairs, these, lanes]
                    own_key = mixed[p + 2 * pairs, these, lanes]
                    scores = lax.dot_general(
                        query, past_key, (((1,), (1,)), ((), ())), preferred_element_type=F32
                    )
                    weights = silu_of_double(scores * live).astype(BF16)
                    total = jnp.dot(weights, past_value, preferred_element_type=F32)
                    own = jnp.sum(
                        query.astype(F32) * own_key.astype(F32), axis=-1, keepdims=True
                    )
                    own = silu_of_double(own * (0.5 * scale))
                    attended[these, at] = total + own * value.astype(F32)
            return 0

        lax.fori_loop(0, pairs, pair, 0)

    def gate_and_add(layer):
        def step(i, _):
            at = pl.ds(pl.multiple_of(i * block_rows, block_rows), block_rows)
            normed[at, :] = (layer_norm(attended[at, :]) * gate[at, :]).astype(BF16)
            return 0

        lax.fori_loop(0, cands // block_rows, step, 0)

        def add(n, _):
            at = pl.ds(pl.multiple_of(n * wide, wide), wide)
            state[:, at] += lax.dot_general(
                normed[...], wout[layer, at, :], (((1,), (1,)), ((), ())), preferred_element_type=F32
            )
            return 0

        lax.fori_loop(0, width // wide, add, 0)

    norm_state()
    arrived(len_in, recv.at[LEN_Z])
    length = len_in[requests[me_c]][:1, :1]
    position = lax.broadcasted_iota(jnp.int32, (1, history), 1)
    live = jnp.where(position < length, 0.5 * scale, 0.0).astype(F32)

    pass_on(in_block, 0, 0)
    pass_on(out_block, 0, 1)
    arrived(win.at[1, :, mine], recv.at[IN1])
    along_z(in_block, 1, 2)
    from_twin(in_block, 0, 0)
    project(0)
    arrived(kv.at[0], recv.at[KV0])
    attend(0, live)
    from_twin(out_block, 0, 1)
    gate_and_add(0)

    norm_state()
    pass_on(in_block, 1, 2)
    from_twin(in_block, 1, 2)
    project(1)
    arrived(kv.at[1], recv.at[KV1])
    attend(1, live)
    gate_and_add(1)

    for j in range(users):
        rank_out[j] = fold(state[part * j : part * (j + 1), :]).astype(BF16)
    for c in plane:
        post(rank_out.at[c], rank_mid.at[me_c], (me_s, c), send.at[RANK_P], recv.at[RANK_P])
    here(rank_out.at[me_c], rank_mid.at[me_c], recv.at[RANK_P])
    arrived(rank_mid, recv.at[RANK_P])
    for s in range(users):
        rank_send[s] = rank_mid[inverse[s]]
    for s in column:
        post(rank_send.at[s], rank_in.at[me_s], (s, me_c), send.at[RANK_Z], recv.at[RANK_Z])
    here(rank_send.at[me_s], rank_in.at[me_s], recv.at[RANK_Z])
    arrived(rank_in, recv.at[RANK_Z])
    for m in range(users // 2):
        both = [unfold(rank_in[2 * m + i].astype(F32)) for i in range(2)]
        out[2 * part * m : 2 * part * (m + 1), :] = jnp.concatenate(both, axis=0).astype(BF16)

    others = pl.ds(0, users - 1)
    arrived(feat_out.at[others], send.at[FEAT_Z])
    arrived(len_out.at[others], send.at[LEN_Z])
    arrived(feat_mid.at[others], send.at[FEAT_P])
    arrived(rank_out.at[others], send.at[RANK_P])
    arrived(rank_send.at[others], send.at[RANK_Z])
    arrived(win.at[0, others, mine], send.at[IN0])
    arrived(win.at[1, others, mine], send.at[IN1])
    arrived(wout.at[:, pl.ds(0, (users - 1) * narrow), mine], send.at[WO])
    arrived(kv.at[0, pl.ds(0, (users - 1) * rows)], send.at[KV0])
    arrived(kv.at[1, pl.ds(0, (users - 1) * rows)], send.at[KV1])
    sent(in_block, 0, 0)
    sent(out_block, 0, 1)
    sent(in_block, 1, 2)


def shards(kv_cache, requests, lengths, cand_feats, w_in, w_out):
    users, layers, rows, _ = kv_cache.shape
    _, part, width = cand_feats.shape
    cands, history = users * part, users * rows
    wide = w_in.shape[2]
    vmem = pl.BlockSpec(memory_space=pltpu.VMEM)
    smem = pl.BlockSpec(memory_space=pltpu.SMEM)
    anywhere = pl.BlockSpec(memory_space=pl.ANY)
    piece = pltpu.VMEM((users, 2 * part, width // 2), BF16)
    flops = layers * (2 * cands * width * 5 * width + 4 * cands * history * width)
    ranked = pl.pallas_call(
        kernel,
        out_shape=jax.ShapeDtypeStruct((cands, width), BF16),
        in_specs=[smem, smem, anywhere, vmem, anywhere, anywhere],
        out_specs=vmem,
        scratch_shapes=[
            pltpu.VMEM((layers, users, width, wide), BF16),
            pltpu.VMEM((layers, width, width), BF16),
            pltpu.VMEM((layers, history, 2 * width), BF16),
            pltpu.VMEM((cands, width), F32),
            pltpu.VMEM((cands, width), BF16),
            pltpu.VMEM((cands, width), F32),
            pltpu.VMEM((3 * width // wide, cands, wide), BF16),
            pltpu.VMEM((cands, width), F32),
            pltpu.VMEM((users, 8, 128), jnp.int32),
            pltpu.VMEM((users, 8, 128), jnp.int32),
            *[piece] * 8,
            pltpu.SMEM((users,), jnp.int32),
            pltpu.SemaphoreType.DMA((10,)),
            pltpu.SemaphoreType.DMA((10,)),
            pltpu.SemaphoreType.DMA((3, 4)),
            pltpu.SemaphoreType.DMA((3, 4)),
            pltpu.SemaphoreType.DMA((3, 5)),
            pltpu.SemaphoreType.DMA((3, 5)),
        ],
        compiler_params=pltpu.CompilerParams(
            collective_id=0, has_side_effects=True, vmem_limit_bytes=60 * 1024 * 1024
        ),
        cost_estimate=pl.CostEstimate(
            flops=flops, bytes_accessed=64 * 1024 * 1024, transcendentals=cands * width * 24
        ),
        name="rank_two_layers",
    )(requests, lengths, kv_cache, cand_feats.reshape(cands, width), w_in, jnp.swapaxes(w_out, 1, 2))
    return ranked.reshape(cand_feats.shape)


def solution(mesh):
    return jax.shard_map(
        shards,
        mesh=mesh,
        in_specs=(
            P("store", None, "cand", None),
            P("store"),
            P("store"),
            P("store", "cand", None),
            P(None, None, "cand"),
            P(None, None, "cand"),
        ),
        out_specs=P("store", "cand", None),
        check_vma=False,
    )
```

time: 509 us -> 205 us (0.40); the launches traced: 501 us -> 202 us
  waiting for transfers between devices: 305 us -> 0 us
  Pallas kernels: 0 us -> 200 us
  local copies, waits for them, and re-layouts: 56.6 us -> 2.07 us
  matrix products: 44.8 us -> 0 us
  blocking collectives: 36.4 us -> 0 us
  starting transfers between devices: 23 us -> 0 us
  other arithmetic: 21.2 us -> 0 us
  between operations: 13.6 us -> 0.01 us
    all_to_all x3 -> x0, waiting for transfers between devices: 304 us -> none  [the longest x1 181 us: shards(): lax.all_to_all(outgoing, 'store', split_axis=0, concat_axis=0, tiled=True)]
    pallas_call x0 -> x1, Pallas kernels: none -> 200 us  [shards(): pl.pallas_call(kernel, out_shape=jax.ShapeDtypeStruct((cands, width), BF1...]
    dot_general x6 -> x0, matrix products: 44.8 us -> none  [the longest x2 19.4 us: attend(): jnp.einsum('ghcj,gjhd->gchd', weights, past_value, preferred_element_type...]
    all_to_all x1 -> x0, blocking collectives: 36.4 us -> none  [shards(): lax.all_to_all(result, 'cand', split_axis=1, concat_axis=0, tiled=True)]
    all_to_all x3 -> x0, starting transfers between devices: 22.8 us -> none  [the longest x1 8.57 us: shards(): lax.all_to_all(outgoing, 'store', split_axis=0, concat_axis=0, tiled=True)]
    slice x7 -> x0, local copies, waits for them, and re-layouts: 20.9 us -> none  [the longest x3 10 us: attend(): past_key = cache[:, :, :width].reshape(group, history, heads, head)]
    unnamed x5 -> x0, other arithmetic: 9.5 us -> none
    all_to_all x1 -> x0, local copies, waits for them, and re-layouts: 8.3 us -> none  [shards(): lax.all_to_all(lax.all_to_all(outgoing, 'store', split_axis=0, concat_axi...]
  transfers between devices with their start and end apart: 7 -> 0, of which waited for: 2 -> 0; matrix products, arithmetic and copies ran while one was open for 21% -> 0% of each run, Pallas kernels for 0% -> 0%
where the time goes in v1:
time: 205 us; the launch traced here: 202 us
  Pallas kernels  200 us (98%)
  local copies, waits for them, and re-layouts  2.07 us (1%)
    pallas_call x1, Pallas kernels, shards(): pl.pallas_call(kernel, out_shape=jax.ShapeDtypeStruct((cands, width), BF1...  200 us

profile of v1, /device:TPU:32, one launch (start us, length us, event | category | flops | bytes accessed | tf_op | source)
XLA Modules:
  0.0 202.4 jit_solution(6169128681283917156)
XLA Ops:
  0.0 200.3 %rank_two_layers.1 = bf16[384,1024]{1,0:T(8,128)(2,1)} custom-call(s32[16]{0:T(128)} %requests.1, s32[16]{0:T(128)} %lengths.1, bf16[16,2,64,2048]{3,2,1,0:T(8,128)(2,1)} %kv_hbm.1, bf16[384,1024]{1,0:T(8,128)(2,1)} %bitcast.4, bf16[2,1024,256]{2,1,0:T(8,128)(2,1)} %win_hbm.1, bf16[2,64,1024]{2,1,0:T(8,128)(2,1)} %bitcast.5), custom_call_target="tpu_custom_call" | custom-call | flops 11274289152 | bytes 67108864 | tf_op jit(solution)/shard_map/rank_two_layers/pallas_call | solution.py:385
  200.3 2.1 %copy.8 = bf16[16,24,1024]{2,1,0:T(8,128)(2,1)} copy(bf16[16,24,1024]{2,1,0:T(8,128)(2,1)} %bitcast.3) | data formatting | bytes 1572864

commit v2 on v1

v2 whole, which is shorter than its diff:
```python
import functools

import jax
import jax.numpy as jnp
from jax import lax
from jax.experimental import pallas as pl
from jax.experimental.pallas import tpu as pltpu
from jax.sharding import PartitionSpec as P

MESH = pl.DeviceIdType.MESH
HEADS = 8
HEAD = 128
SIDE = 4
DEPTH = 8
LOW = 8
CORES = 2
F32 = jnp.float32
BF16 = jnp.bfloat16

PLANE = (
    ((1, 0), (3, 0), (0, 1), (0, 3))
    + ((1, 1), (3, 3), (1, 3), (3, 1))
    + ((2, 2), (2, 0), (0, 2))
    + ((2, 1), (2, 3), (1, 2), (3, 2))
)
COLUMN = tuple((dz, dk) for dz in (4, 3, 5, 2, 6, 1, 7) for dk in (0, 1)) + ((0, 1),)


def layer_norm(values):
    mean = jnp.mean(values, axis=-1, keepdims=True)
    centred = values - mean
    spread = jnp.mean(centred * centred, axis=-1, keepdims=True)
    return centred * lax.rsqrt(spread + 1e-06)


def silu_of_double(half):
    return half + half * jnp.tanh(half)


def fold(rows):
    half = rows.shape[1] // 2
    return jnp.concatenate([rows[:, :half], rows[:, half:]], axis=0)


def unfold(piece):
    half = piece.shape[0] // 2
    return jnp.concatenate([piece[:half], piece[half:]], axis=1)


def arrived(region, sem):
    pltpu.make_async_copy(region, region, sem).wait()


def kernel(
    requests,
    lengths,
    kv_hbm,
    feats,
    win_hbm,
    wout_hbm,
    out,
    win,
    wout,
    kv,
    state,
    normed,
    gate,
    mixed,
    attended,
    len_out,
    len_in,
    feat_out,
    feat_in,
    feat_mid,
    feat_here,
    rank_out,
    rank_send,
    rank_in,
    inverse,
    send,
    recv,
    a_send,
    a_recv,
    b_send,
    b_recv,
    z_send,
    z_recv,
    twin_send,
    twin_recv,
    *rank_mid,
):
    me_s = lax.axis_index("store")
    me_c = lax.axis_index("cand")
    z, core = me_s // CORES, lax.rem(me_s, CORES)
    x, y = me_c // SIDE, lax.rem(me_c, SIDE)
    layers, history, _ = kv.shape
    cands, width = state.shape
    users = kv_hbm.shape[0]
    part = cands // users
    tiles = part // LOW
    tall = users * LOW
    rows = history // users
    wide = win.shape[4]
    narrow = wout_hbm.shape[1]

    plane = [
        lax.rem(x + dx, SIDE) * SIDE + lax.rem(y + dy, SIDE) for dx, dy in PLANE
    ]
    column = [
        lax.rem(z + dz, DEPTH) * CORES + lax.rem(core + dk, CORES) for dz, dk in COLUMN
    ]
    barrier = pltpu.get_barrier_semaphore()
    for c in plane:
        pl.semaphore_signal(barrier, inc=1, device_id=(me_s, c), device_id_type=MESH)
    for s in column:
        pl.semaphore_signal(barrier, inc=1, device_id=(s, me_c), device_id_type=MESH)
    for o in range(users):
        len_out[o] = jnp.full((8, 128), lengths[o], jnp.int32)
    pl.semaphore_wait(barrier, len(plane) + len(column))

    def post(src, dst, device, send_sem, recv_sem):
        pltpu.make_async_remote_copy(
            src, dst, send_sem, recv_sem, device_id=device, device_id_type=MESH
        ).start()

    def here(src, dst, sem):
        pltpu.make_async_copy(src, dst, sem).start()

    FEAT_Z, LEN_Z, FEAT_P, KV0, KEY1, VALUE1, KEY1_LAST, VALUE1_LAST, RANK_P = range(9)
    RANK_Z = RANK_P + tiles
    early = width - wide
    IN0, WO, IN1 = range(3)

    depth = width // SIDE // CORES
    quarter = lax.rem(z, SIDE)

    def span(q, k, start=0, size=depth):
        return pl.ds(pl.multiple_of((q * CORES + k) * depth + start, size), size)

    rows_here = pl.ds(pl.multiple_of(me_c * rows, rows), rows)
    steps = (1, 3, 2)
    x_peers = [lax.rem(x + d, SIDE) * SIDE + y for d in steps]
    y_peers = [x * SIDE + lax.rem(y + d, SIDE) for d in steps]
    x_from = [lax.rem(x + SIDE - d, SIDE) for d in steps]
    y_from = [lax.rem(y + SIDE - d, SIDE) for d in steps]
    every = slice(None)

    def share(group, axis, at_x, at_y):
        if group == WO:
            low = narrow // 2
            return wout.at[:, at_x, at_y, pl.ds(axis * low, low), span(quarter, core)]
        low = depth // 2
        return win.at[group // 2, at_x, at_y, span(quarter, core, axis * low, low)]

    def source(group, axis):
        if group == WO:
            low = narrow // 2
            return wout_hbm.at[:, pl.ds(axis * low, low), span(quarter, core)]
        low = depth // 2
        return win_hbm.at[group // 2, span(quarter, core, axis * low, low)]

    def line(group, axis):
        return share(group, axis, every, y) if axis == 0 else share(group, axis, x, every)

    def spread_first(group):
        for axis, peers in enumerate((x_peers, y_peers)):
            src, dst = source(group, axis), share(group, axis, x, y)
            for c in peers:
                post(src, dst, (me_s, c), a_send.at[group, axis], a_recv.at[group, axis])
            here(src, dst, a_recv.at[group, axis])

    def spread_second(group):
        for axis, peers in enumerate((y_peers, x_peers)):
            ref = line(group, axis)
            arrived(ref, a_recv.at[group, axis])
            for i, c in enumerate(peers):
                post(ref, ref, (me_s, c), b_send.at[group, axis, i], b_recv.at[group, axis, i])

    def spread_end(group):
        for i in range(len(steps)):
            arrived(share(group, 0, every, y_from[i]), b_recv.at[group, 0, i])
            arrived(share(group, 1, x_from[i], every), b_recv.at[group, 1, i])

    def spread_sent(group):
        most = pl.ds(0, SIDE - 1)
        arrived(share(group, 0, most, y), a_send.at[group, 0])
        arrived(share(group, 1, x, most), a_send.at[group, 1])
        for i in range(len(steps)):
            arrived(line(group, 0), b_send.at[group, 0, i])
            arrived(line(group, 1), b_send.at[group, 1, i])

    def histories(layer, number, first, size):
        lanes = pl.ds(first, size)
        dst = kv.at[layer, rows_here, lanes]
        for c in plane:
            src = kv_hbm.at[c, layer, :, lanes]
            post(src, dst, (me_s, c), send.at[number], recv.at[number])
        here(kv_hbm.at[me_c, layer, :, lanes], dst, recv.at[number])

    def histories_sent(layer, number, first, size):
        lanes = pl.ds(first, size)
        arrived(kv.at[layer, pl.ds(0, (users - 1) * rows), lanes], send.at[number])

    up, down = lax.rem(z + 1, DEPTH) * CORES, lax.rem(z + DEPTH - 1, DEPTH) * CORES
    twin = z * CORES + 1 - core
    ahead, behind, across = (lax.rem(quarter + d, SIDE) for d in (1, 3, 2))
    low, high = pl.ds(0, SIDE // 2), pl.ds(SIDE // 2, SIDE // 2)

    def block(group, q, k, part_of=every):
        if group == WO:
            return wout.at[:, part_of, :, :, span(q, k)]
        return win.at[group // 2, part_of, :, span(q, k)]

    def along(ref, to, group, i):
        post(ref, ref, (to + core, me_c), z_send.at[group, i], z_recv.at[group, i])

    def to_twin(ref, group, i):
        post(ref, ref, (twin, me_c), twin_send.at[group, i], twin_recv.at[group, i])

    def z_first(group):
        ref = block(group, quarter, core)
        along(ref, up, group, 0)
        along(ref, down, group, 1)
        to_twin(ref, group, 0)

    def z_second(group):
        for i, (q, to, part_of) in enumerate(((behind, up, low), (ahead, down, high))):
            arrived(block(group, q, core), z_recv.at[group, i])
            along(block(group, q, core, part_of), to, group, 2 + i)
            to_twin(block(group, q, core), group, 1 + i)

    def z_end(group):
        for i, part_of in enumerate((low, high)):
            ref = block(group, across, core, part_of)
            arrived(ref, z_recv.at[group, 2 + i])
            to_twin(ref, group, 3 + i)

    def from_twin(group):
        for i, (q, part_of) in enumerate(
            ((quarter, every), (behind, every), (ahead, every), (across, low), (across, high))
        ):
            arrived(block(group, q, 1 - core, part_of), twin_recv.at[group, i])

    def z_sent(group):
        whole, part_of = block(group, quarter, core), block(group, quarter, core, low)
        for i in range(4):
            arrived(whole if i < 2 else part_of, z_send.at[group, i])
        for i in range(5):
            arrived(whole if i < 3 else part_of, twin_send.at[group, i])

    spread_first(IN0)
    spread_first(WO)

    for m in range(users // 2):
        both = feats[2 * part * m : 2 * part * (m + 1), :].astype(F32)
        for i in range(2):
            for t in range(tiles):
                first = part * i + LOW * t
                feat_out[2 * m + i, 2 * LOW * t : 2 * LOW * (t + 1), :] = fold(
                    both[first : first + LOW]
                ).astype(BF16)
    for s in column:
        post(feat_out.at[s], feat_in.at[me_s], (s, me_c), send.at[FEAT_Z], recv.at[FEAT_Z])
    here(feat_out.at[me_s], feat_in.at[me_s], recv.at[FEAT_Z])
    for s in column:
        post(len_out.at[s], len_in.at[me_s], (s, me_c), send.at[LEN_Z], recv.at[LEN_Z])
    here(len_out.at[me_s], len_in.at[me_s], recv.at[LEN_Z])

    spread_second(IN0)
    spread_first(IN1)
    spread_second(WO)
    spread_end(IN0)
    z_first(IN0)
    spread_second(IN1)
    histories(0, KV0, 0, 2 * width)
    spread_end(WO)
    z_first(WO)
    spread_end(IN1)

    arrived(feat_in, recv.at[FEAT_Z])
    for k in range(users):
        feat_mid[k] = feat_in[requests[k]]
    for c in plane:
        post(feat_mid.at[c], feat_here.at[me_c], (me_s, c), send.at[FEAT_P], recv.at[FEAT_P])
    here(feat_mid.at[me_c], feat_here.at[me_c], recv.at[FEAT_P])

    for s in range(users):
        at = 0
        for k in range(users):
            at = jnp.where(requests[k] == s, k, at)
        inverse[s] = at

    arrived(feat_here, recv.at[FEAT_P])
    for j in range(users):
        for t in range(tiles):
            state[tall * t + LOW * j : tall * t + LOW * (j + 1), :] = unfold(
                feat_here[j, 2 * LOW * t : 2 * LOW * (t + 1), :].astype(F32)
            )

    block_rows = 32

    def norm_state():
        def step(i, _):
            at = pl.ds(pl.multiple_of(i * block_rows, block_rows), block_rows)
            normed[at, :] = layer_norm(state[at, :]).astype(BF16)
            return 0

        lax.fori_loop(0, cands // block_rows, step, 0)

    def project(layer):
        blocks = width // wide

        def gates(j, _):
            acc = jnp.dot(normed[...], win[layer, 0, j], preferred_element_type=F32)
            at = pl.ds(pl.multiple_of(j * wide, wide), wide)
            gate[:, at] = silu_of_double(0.5 * acc)
            return 0

        lax.fori_loop(0, blocks, gates, 0)

        def others(j, _):
            acc = jnp.dot(normed[...], win[layer, 1 + j // SIDE, lax.rem(j, SIDE)], preferred_element_type=F32)
            mixed[j] = silu_of_double(0.5 * acc).astype(BF16)
            return 0

        lax.fori_loop(0, 3 * blocks, others, 0)

    scale = HEAD ** (-0.5)
    pairs = width // wide

    def attend_pair(layer, p, which):
        for i in range(wide // HEAD):
            lanes = slice(i * HEAD, (i + 1) * HEAD)
            at = pl.ds(pl.multiple_of(p * wide + i * HEAD, HEAD), HEAD)
            at_value = pl.ds(pl.multiple_of(width + p * wide + i * HEAD, HEAD), HEAD)
            past_key = kv[layer, :, at]
            past_value = kv[layer, :, at_value]
            for t in which:
                these = slice(t * tall, (t + 1) * tall)
                value = mixed[p, these, lanes]
                query = mixed[p + pairs, these, lanes]
                own_key = mixed[p + 2 * pairs, these, lanes]
                scores = lax.dot_general(
                    query, past_key, (((1,), (1,)), ((), ())), preferred_element_type=F32
                )
                weights = silu_of_double(scores * live).astype(BF16)
                total = jnp.dot(weights, past_value, preferred_element_type=F32)
                own = jnp.sum(query.astype(F32) * own_key.astype(F32), axis=-1, keepdims=True)
                own = silu_of_double(own * (0.5 * scale))
                attended[these, at] = total + own * value.astype(F32)

    def attend(layer, count):
        def step(p, _):
            attend_pair(layer, p, range(tiles))
            return 0

        lax.fori_loop(0, count, step, 0)

    def gate_and_add(layer, first, size):
        def step(i, _):
            at = pl.ds(pl.multiple_of(first + i * block_rows, block_rows), block_rows)
            normed[at, :] = (layer_norm(attended[at, :]) * gate[at, :]).astype(BF16)
            return 0

        lax.fori_loop(0, size // block_rows, step, 0)
        these = slice(first, first + size)

        def add(n, _):
            at = pl.ds(pl.multiple_of(n * wide, wide), wide)
            columns = wout[layer, n].reshape(wide, width)
            state[these, at] += lax.dot_general(
                normed[these, :], columns, (((1,), (1,)), ((), ())), preferred_element_type=F32
            )
            return 0

        lax.fori_loop(0, width // wide, add, 0)

    norm_state()
    arrived(len_in, recv.at[LEN_Z])
    length = len_in[requests[me_c]][:1, :1]
    position = lax.broadcasted_iota(jnp.int32, (1, history), 1)
    live = jnp.where(position < length, 0.5 * scale, 0.0).astype(F32)

    histories(1, KEY1, 0, early)
    histories(1, VALUE1, width, early)
    histories(1, KEY1_LAST, early, wide)
    histories(1, VALUE1_LAST, width + early, wide)

    z_second(IN0)
    z_second(WO)
    z_end(IN0)
    z_first(IN1)
    from_twin(IN0)
    project(0)
    z_end(WO)
    arrived(kv.at[0], recv.at[KV0])
    attend(0, pairs)
    from_twin(WO)
    gate_and_add(0, 0, cands)

    z_second(IN1)
    norm_state()
    z_end(IN1)
    from_twin(IN1)
    project(1)
    arrived(kv.at[1, :, pl.ds(0, early)], recv.at[KEY1])
    arrived(kv.at[1, :, pl.ds(width, early)], recv.at[VALUE1])
    attend(1, pairs - 1)
    arrived(kv.at[1, :, pl.ds(early, wide)], recv.at[KEY1_LAST])
    arrived(kv.at[1, :, pl.ds(width + early, wide)], recv.at[VALUE1_LAST])

    def back(t):
        for j in range(users):
            rank_out[t, j] = fold(state[tall * t + LOW * j : tall * t + LOW * (j + 1), :]).astype(BF16)
        for c in plane:
            post(rank_out.at[t, c], rank_mid[t].at[me_c], (me_s, c), send.at[RANK_P + t], recv.at[RANK_P + t])
        here(rank_out.at[t, me_c], rank_mid[t].at[me_c], recv.at[RANK_P + t])

    def home(t):
        arrived(rank_mid[t], recv.at[RANK_P + t])
        for s in range(users):
            rank_send[t, s] = rank_mid[t][inverse[s]]
        for s in column:
            post(rank_send.at[t, s], rank_in.at[t, me_s], (s, me_c), send.at[RANK_Z + t], recv.at[RANK_Z + t])
        here(rank_send.at[t, me_s], rank_in.at[t, me_s], recv.at[RANK_Z + t])

    for t in range(tiles):
        attend_pair(1, pairs - 1, (t,))
        gate_and_add(1, t * tall, tall)
        back(t)
        if t > 0:
            home(t - 1)
    home(tiles - 1)
    for t in range(tiles):
        arrived(rank_in.at[t], recv.at[RANK_Z + t])
    for m in range(users // 2):
        both = [
            unfold(rank_in[t, 2 * m + i].astype(F32)) for i in range(2) for t in range(tiles)
        ]
        out[2 * part * m : 2 * part * (m + 1), :] = jnp.concatenate(both, axis=0).astype(BF16)

    others = pl.ds(0, users - 1)
    arrived(feat_out.at[others], send.at[FEAT_Z])
    arrived(len_out.at[others], send.at[LEN_Z])
    arrived(feat_mid.at[others], send.at[FEAT_P])
    for t in range(tiles):
        arrived(rank_out.at[t, others], send.at[RANK_P + t])
        arrived(rank_send.at[t, others], send.at[RANK_Z + t])
    histories_sent(0, KV0, 0, 2 * width)
    histories_sent(1, KEY1, 0, early)
    histories_sent(1, VALUE1, width, early)
    histories_sent(1, KEY1_LAST, early, wide)
    histories_sent(1, VALUE1_LAST, width + early, wide)
    for group in (IN0, WO, IN1):
        spread_sent(group)
        z_sent(group)


def shards(kv_cache, requests, lengths, cand_feats, w_in, w_out):
    users, layers, rows, _ = kv_cache.shape
    _, part, width = cand_feats.shape
    cands, history = users * part, users * rows
    wide = w_in.shape[2]
    vmem = pl.BlockSpec(memory_space=pltpu.VMEM)
    smem = pl.BlockSpec(memory_space=pltpu.SMEM)
    anywhere = pl.BlockSpec(memory_space=pl.ANY)
    piece = pltpu.VMEM((users, 2 * part, width // 2), BF16)
    tiles = part // LOW
    tile = pltpu.VMEM((tiles, users, 2 * LOW, width // 2), BF16)
    flops = layers * (2 * cands * width * 5 * width + 4 * cands * history * width)
    ranked = pl.pallas_call(
        kernel,
        out_shape=jax.ShapeDtypeStruct((cands, width), BF16),
        in_specs=[smem, smem, anywhere, vmem, anywhere, anywhere],
        out_specs=vmem,
        scratch_shapes=[
            pltpu.VMEM((layers, SIDE, SIDE, width, wide), BF16),
            pltpu.VMEM((layers, SIDE, SIDE, width // users, width), BF16),
            pltpu.VMEM((layers, history, 2 * width), BF16),
            pltpu.VMEM((cands, width), F32),
            pltpu.VMEM((cands, width), BF16),
            pltpu.VMEM((cands, width), F32),
            pltpu.VMEM((3 * width // wide, cands, wide), BF16),
            pltpu.VMEM((cands, width), F32),
            pltpu.VMEM((users, 8, 128), jnp.int32),
            pltpu.VMEM((users, 8, 128), jnp.int32),
            *[piece] * 4,
            *[tile] * 3,
            pltpu.SMEM((users,), jnp.int32),
            pltpu.SemaphoreType.DMA((9 + 2 * tiles,)),
            pltpu.SemaphoreType.DMA((9 + 2 * tiles,)),
            pltpu.SemaphoreType.DMA((3, 2)),
            pltpu.SemaphoreType.DMA((3, 2)),
            pltpu.SemaphoreType.DMA((3, 2, 3)),
            pltpu.SemaphoreType.DMA((3, 2, 3)),
            pltpu.SemaphoreType.DMA((3, 4)),
            pltpu.SemaphoreType.DMA((3, 4)),
            pltpu.SemaphoreType.DMA((3, 5)),
            pltpu.SemaphoreType.DMA((3, 5)),
            *[pltpu.VMEM((users, 2 * LOW, width // 2), BF16)] * tiles,
        ],
        compiler_params=pltpu.CompilerParams(
            collective_id=0, has_side_effects=True, vmem_limit_bytes=60 * 1024 * 1024
        ),
        cost_estimate=pl.CostEstimate(
            flops=flops, bytes_accessed=64 * 1024 * 1024, transcendentals=cands * width * 24
        ),
        name="rank_two_layers",
    )(requests, lengths, kv_cache, cand_feats.reshape(cands, width), w_in, jnp.swapaxes(w_out, 1, 2))
    return ranked.reshape(cand_feats.shape)


def solution(mesh):
    return jax.shard_map(
        shards,
        mesh=mesh,
        in_specs=(
            P("store", None, "cand", None),
            P("store"),
            P("store"),
            P("store", "cand", None),
            P(None, None, "cand"),
            P(None, None, "cand"),
        ),
        out_specs=P("store", "cand", None),
        check_vma=False,
    )
```

time: 205 us -> 192 us (0.937)
  Pallas kernels: 200 us -> 188 us
    pallas_call x1, Pallas kernels: 200 us -> 188 us  [shards(): pl.pallas_call(kernel, out_shape=jax.ShapeDtypeStruct((cands, width), BF1...]
where the time goes in v2:
time: 192 us; the launch traced here: 190 us
  Pallas kernels  188 us (98%)
  local copies, waits for them, and re-layouts  2.07 us (1%)
    pallas_call x1, Pallas kernels, shards(): pl.pallas_call(kernel, out_shape=jax.ShapeDtypeStruct((cands, width), BF1...  188 us

profile of v2, /device:TPU:32, one launch (start us, length us, event | category | flops | bytes accessed | tf_op | source)
XLA Modules:
  0.0 189.8 jit_solution(12445259878919111079)
XLA Ops:
  0.0 187.8 %rank_two_layers.1 = bf16[384,1024]{1,0:T(8,128)(2,1)} custom-call(s32[16]{0:T(128)} %requests.1, s32[16]{0:T(128)} %lengths.1, bf16[16,2,64,2048]{3,2,1,0:T(8,128)(2,1)} %kv_hbm.1, bf16[384,1024]{1,0:T(8,128)(2,1)} %bitcast.4, bf16[2,1024,256]{2,1,0:T(8,128)(2,1)} %win_hbm.1, bf16[2,64,1024]{2,1,0:T(8,128)(2,1)} %bitcast.5), custom_call_target="tpu_custom_call" | custom-call | flops 11274289152 | bytes 67108864 | tf_op jit(solution)/shard_map/rank_two_layers/pallas_call | solution.py:471
  187.8 2.1 %copy.8 = bf16[16,24,1024]{2,1,0:T(8,128)(2,1)} copy(bf16[16,24,1024]{2,1,0:T(8,128)(2,1)} %bitcast.3) | data formatting | bytes 1572864

commit v3 on v2

--- a/solution.py
+++ b/solution.py
@@ -272,11 +272,11 @@
     spread_end(IN0)
     z_first(IN0)
     spread_second(IN1)
-    histories(0, KV0, 0, 2 * width)
     spread_end(WO)
     z_first(WO)
     spread_end(IN1)
 
+    histories(0, KV0, 0, 2 * width)
     arrived(feat_in, recv.at[FEAT_Z])
     for k in range(users):
         feat_mid[k] = feat_in[requests[k]]
@@ -289,6 +289,15 @@
         for k in range(users):
             at = jnp.where(requests[k] == s, k, at)
         inverse[s] = at
+
+    z_second(IN0)
+    z_first(IN1)
+    z_second(WO)
+    histories(1, KEY1, 0, early)
+    histories(1, VALUE1, width, early)
+    histories(1, KEY1_LAST, early, wide)
+    histories(1, VALUE1_LAST, width + early, wide)
+    z_end(IN0)
 
     arrived(feat_here, recv.at[FEAT_P])
     for j in range(users):
@@ -381,24 +390,15 @@
     position = lax.broadcasted_iota(jnp.int32, (1, history), 1)
     live = jnp.where(position < length, 0.5 * scale, 0.0).astype(F32)
 
-    histories(1, KEY1, 0, early)
-    histories(1, VALUE1, width, early)
-    histories(1, KEY1_LAST, early, wide)
-    histories(1, VALUE1_LAST, width + early, wide)
-
-    z_second(IN0)
-    z_second(WO)
-    z_end(IN0)
-    z_first(IN1)
     from_twin(IN0)
     project(0)
     z_end(WO)
+    z_second(IN1)
     arrived(kv.at[0], recv.at[KV0])
     attend(0, pairs)
     from_twin(WO)
     gate_and_add(0, 0, cands)
 
-    z_second(IN1)
     norm_state()
     z_end(IN1)
     from_twin(IN1)

time: 192 us -> 169 us (0.88)
  Pallas kernels: 188 us -> 164 us
    pallas_call x1, Pallas kernels: 188 us -> 164 us  [shards(): pl.pallas_call(kernel, out_shape=jax.ShapeDtypeStruct((cands, width), BF1...]
where the time goes in v3:
time: 169 us; the launch traced here: 166 us
  Pallas kernels  164 us (97%)
  local copies, waits for them, and re-layouts  2.07 us (1%)
    pallas_call x1, Pallas kernels, shards(): pl.pallas_call(kernel, out_shape=jax.ShapeDtypeStruct((cands, width), BF1...  164 us

profile of v3, /device:TPU:32, one launch (start us, length us, event | category | flops | bytes accessed | tf_op | source)
XLA Modules:
  0.0 166.0 jit_solution(9907307899246015692)
XLA Ops:
  0.0 163.9 %rank_two_layers.1 = bf16[384,1024]{1,0:T(8,128)(2,1)} custom-call(s32[16]{0:T(128)} %requests.1, s32[16]{0:T(128)} %lengths.1, bf16[16,2,64,2048]{3,2,1,0:T(8,128)(2,1)} %kv_hbm.1, bf16[384,1024]{1,0:T(8,128)(2,1)} %bitcast.4, bf16[2,1024,256]{2,1,0:T(8,128)(2,1)} %win_hbm.1, bf16[2,64,1024]{2,1,0:T(8,128)(2,1)} %bitcast.5), custom_call_target="tpu_custom_call" | custom-call | flops 11274289152 | bytes 67108864 | tf_op jit(solution)/shard_map/rank_two_layers/pallas_call | solution.py:471
  163.9 2.1 %copy.8 = bf16[16,24,1024]{2,1,0:T(8,128)(2,1)} copy(bf16[16,24,1024]{2,1,0:T(8,128)(2,1)} %bitcast.3) | data formatting | bytes 1572864

commit v4 on v3

--- a/solution.py
+++ b/solution.py
@@ -276,13 +276,17 @@
     z_first(WO)
     spread_end(IN1)
 
-    histories(0, KV0, 0, 2 * width)
+    for first in (0, width):
+        histories(0, KV0, first, width // 2)
     arrived(feat_in, recv.at[FEAT_Z])
     for k in range(users):
         feat_mid[k] = feat_in[requests[k]]
     for c in plane:
         post(feat_mid.at[c], feat_here.at[me_c], (me_s, c), send.at[FEAT_P], recv.at[FEAT_P])
     here(feat_mid.at[me_c], feat_here.at[me_c], recv.at[FEAT_P])
+
+    for first in (width // 2, width + width // 2):
+        histories(0, KV0, first, width // 2)
 
     for s in range(users):
         at = 0

time: 169 us -> 164 us (0.970)
  Pallas kernels: 164 us -> 160 us
    pallas_call x1, Pallas kernels: 164 us -> 160 us  [shards(): pl.pallas_call(kernel, out_shape=jax.ShapeDtypeStruct((cands, width), BF1...]
where the time goes in v4:
time: 164 us; the launch traced here: 162 us
  Pallas kernels  160 us (98%)
  local copies, waits for them, and re-layouts  2.07 us (1%)
    pallas_call x1, Pallas kernels, shards(): pl.pallas_call(kernel, out_shape=jax.ShapeDtypeStruct((cands, width), BF1...  160 us

profile of v4, /device:TPU:32, one launch (start us, length us, event | category | flops | bytes accessed | tf_op | source)
XLA Modules:
  0.0 162.1 jit_solution(7698719609489585312)
XLA Ops:
  0.0 160.0 %rank_two_layers.1 = bf16[384,1024]{1,0:T(8,128)(2,1)} custom-call(s32[16]{0:T(128)} %requests.1, s32[16]{0:T(128)} %lengths.1, bf16[16,2,64,2048]{3,2,1,0:T(8,128)(2,1)} %kv_hbm.1, bf16[384,1024]{1,0:T(8,128)(2,1)} %bitcast.4, bf16[2,1024,256]{2,1,0:T(8,128)(2,1)} %win_hbm.1, bf16[2,64,1024]{2,1,0:T(8,128)(2,1)} %bitcast.5), custom_call_target="tpu_custom_call" | custom-call | flops 11274289152 | bytes 67108864 | tf_op jit(solution)/shard_map/rank_two_layers/pallas_call | solution.py:475
  160.0 2.1 %copy.8 = bf16[16,24,1024]{2,1,0:T(8,128)(2,1)} copy(bf16[16,24,1024]{2,1,0:T(8,128)(2,1)} %bitcast.3) | data formatting | bytes 1572864

commit v5 on v4

--- a/solution.py
+++ b/solution.py
@@ -55,7 +55,7 @@
     requests,
     lengths,
     kv_hbm,
-    feats,
+    feats_hbm,
     win_hbm,
     wout_hbm,
     out,
@@ -87,6 +87,8 @@
     z_recv,
     twin_send,
     twin_recv,
+    feats,
+    feats_sem,
     *rank_mid,
 ):
     me_s = lax.axis_index("store")
@@ -109,6 +111,8 @@
     column = [
         lax.rem(z + dz, DEPTH) * CORES + lax.rem(core + dk, CORES) for dz, dk in COLUMN
     ]
+    feats_copy = pltpu.make_async_copy(feats_hbm, feats, feats_sem)
+    feats_copy.start()
     barrier = pltpu.get_barrier_semaphore()
     for c in plane:
         pl.semaphore_signal(barrier, inc=1, device_id=(me_s, c), device_id_type=MESH)
@@ -251,6 +255,7 @@
     spread_first(IN0)
     spread_first(WO)
 
+    feats_copy.wait()
     for m in range(users // 2):
         both = feats[2 * part * m : 2 * part * (m + 1), :].astype(F32)
         for i in range(2):
@@ -437,11 +442,16 @@
     home(tiles - 1)
     for t in range(tiles):
         arrived(rank_in.at[t], recv.at[RANK_Z + t])
-    for m in range(users // 2):
-        both = [
-            unfold(rank_in[t, 2 * m + i].astype(F32)) for i in range(2) for t in range(tiles)
-        ]
-        out[2 * part * m : 2 * part * (m + 1), :] = jnp.concatenate(both, axis=0).astype(BF16)
+        for o in range(users):
+            first = part * o + LOW * t
+            state[first : first + LOW, :] = unfold(rank_in[t, o].astype(F32))
+
+    def cast(i, _):
+        at = pl.ds(pl.multiple_of(i * block_rows, block_rows), block_rows)
+        out[at, :] = state[at, :].astype(BF16)
+        return 0
+
+    lax.fori_loop(0, cands // block_rows, cast, 0)
 
     others = pl.ds(0, users - 1)
     arrived(feat_out.at[others], send.at[FEAT_Z])
@@ -475,7 +485,7 @@
     ranked = pl.pallas_call(
         kernel,
         out_shape=jax.ShapeDtypeStruct((cands, width), BF16),
-        in_specs=[smem, smem, anywhere, vmem, anywhere, anywhere],
+        in_specs=[smem, smem, anywhere, anywhere, anywhere, anywhere],
         out_specs=vmem,
         scratch_shapes=[
             pltpu.VMEM((layers, SIDE, SIDE, width, wide), BF16),
@@ -501,6 +511,8 @@
             pltpu.SemaphoreType.DMA((3, 4)),
             pltpu.SemaphoreType.DMA((3, 5)),
             pltpu.SemaphoreType.DMA((3, 5)),
+            pltpu.VMEM((cands, width), BF16),
+            pltpu.SemaphoreType.DMA,
             *[pltpu.VMEM((users, 2 * LOW, width // 2), BF16)] * tiles,
         ],
         compiler_params=pltpu.CompilerParams(

time: 164 us -> 163 us (level)
  no operation moved by 1% of the time
where the time goes in v5:
time: 163 us; the launch traced here: 162 us
  Pallas kernels  160 us (98%)
  local copies, waits for them, and re-layouts  2.07 us (1%)
    pallas_call x1, Pallas kernels, shards(): pl.pallas_call(kernel, out_shape=jax.ShapeDtypeStruct((cands, width), BF1...  160 us

profile of v5, /device:TPU:32, one launch (start us, length us, event | category | flops | bytes accessed | tf_op | source)
XLA Modules:
  0.0 161.7 jit_solution(8901684358970788648)
XLA Ops:
  0.0 159.6 %rank_two_layers.1 = bf16[384,1024]{1,0:T(8,128)(2,1)} custom-call(s32[16]{0:T(128)} %requests.1, s32[16]{0:T(128)} %lengths.1, bf16[16,2,64,2048]{3,2,1,0:T(8,128)(2,1)} %kv_hbm.1, bf16[384,1024]{1,0:T(8,128)(2,1)} %bitcast.4, bf16[2,1024,256]{2,1,0:T(8,128)(2,1)} %win_hbm.1, bf16[2,64,1024]{2,1,0:T(8,128)(2,1)} %bitcast.5), custom_call_target="tpu_custom_call" | custom-call | flops 11274289152 | bytes 67108864 | tf_op jit(solution)/shard_map/rank_two_layers/pallas_call | solution.py:485
  159.6 2.1 %copy.8 = bf16[16,24,1024]{2,1,0:T(8,128)(2,1)} copy(bf16[16,24,1024]{2,1,0:T(8,128)(2,1)} %bitcast.3) | data formatting | bytes 1572864
